TPU v7x, 32 devices: a whole 2x2x4 slice. The times are simulated.
32 devices in a mesh: section: 2 (over core), batch: 16 (over z, y, x).
Axes of the slice: x: 2, y: 2, z: 4, core: 2. Of those that a mesh axis runs over, the one named last changes fastest.
Arguments:
- tokens: bfloat16 [16384, 768], P('batch'), may hold values from -6 to 6
- cotangent: bfloat16 [16384, 768], P('batch'), may hold values from -6 to 6
- sentence_ids: int32 [16384], P('batch'), may hold values from 0 to 3, as said below
- query_weight: bfloat16 [2, 768, 768], P('section'), may hold values from -0.21875 to 0.21875
- query_bias: float32 [2, 768], P('section'), may hold values from -1.8 to 1.8
- keys_weight: bfloat16 [2, 768, 768], P('section'), may hold values from -0.21875 to 0.21875
- value_weight: bfloat16 [2, 768, 768], P('section'), may hold values from -0.21875 to 0.21875
- value_bias: float32 [2, 768], P('section'), may hold values from -1.8 to 1.8
- mixer_weight: bfloat16 [2, 768, 768], P('section'), may hold values from -0.875 to 0.875
- mixer_bias: float32 [2, 768], P('section'), may hold values from -1.8 to 1.8
- first_gain: float32 [2, 768], P('section'), may hold values from 0.5 to 1.5
- first_shift: float32 [2, 768], P('section'), may hold values from -1.8 to 1.8
- expand_weight: bfloat16 [2, 768, 3072], P('section'), may hold values from -0.21875 to 0.21875
- expand_bias: float32 [2, 3072], P('section'), may hold values from -1.8 to 1.8
- shrink_weight: bfloat16 [2, 3072, 768], P('section'), may hold values from -0.109375 to 0.109375
- shrink_bias: float32 [2, 768], P('section'), may hold values from -1.8 to 1.8
- second_gain: float32 [2, 768], P('section'), may hold values from 0.5 to 1.5
- second_shift: float32 [2, 768], P('section'), may hold values from -1.8 to 1.8
Outputs:
- layer_out: bfloat16 [2, 16384, 768], P('section', 'batch')
- layer_in_grad: bfloat16 [2, 16384, 768], P('section', 'batch')
- query_dweight: float32 [2, 768, 768], P('section')
- query_dbias: float32 [2, 768], P('section')
- keys_dweight: float32 [2, 768, 768], P('section')
- value_dweight: float32 [2, 768, 768], P('section')
- value_dbias: float32 [2, 768], P('section')
- mixer_dweight: float32 [2, 768, 768], P('section')
- mixer_dbias: float32 [2, 768], P('section')
- first_dgain: float32 [2, 768], P('section')
- first_dshift: float32 [2, 768], P('section')
- expand_dweight: float32 [2, 768, 3072], P('section')
- expand_dbias: float32 [2, 3072], P('section')
- shrink_dweight: float32 [2, 3072, 768], P('section')
- shrink_dbias: float32 [2, 768], P('section')
- second_dgain: float32 [2, 768], P('section')
- second_dshift: float32 [2, 768], P('section')
Inputs may be any that keep to these rules, and one draw needn't show every extreme that they name: Within each aligned block of 512 tokens of sentence_ids, counted from the start, the ids number whole sentences in order from 0; each sentence holds 128, 256 or 512 tokens. Tokens attend only to tokens of the same block with the same id.
All inputs are finite; a program needn't handle non-finite values.
Results may differ from a plain program's by a relative error of at most 0.02.
Values may be sent and summed in bfloat16 or wider, within the bound.
A program may use at most 256 MiB of HBM per device.

v0:
```python
import jax
import jax.numpy as jnp
from jax import lax
from jax.sharding import PartitionSpec as P

HEADS = 12
HEAD_DIM = 64
ROWS = 512


epsilon = 1e-06
root_half = 0.7071067811865476
inv_root_tau = 0.3989422804014327


def passed_along(shard, axis, by):
    length = lax.axis_size(axis)
    pairs = [(i, i + by) for i in range(length) if 0 <= i + by < length]
    return lax.ppermute(shard, axis, pairs)


def product(left_side, right_side):
    return jnp.dot(left_side, right_side, preferred_element_type=jnp.float32)


def product_left(left_side, right_side):
    return lax.dot_general(
        left_side, right_side, (((0,), (0,)), ((), ())), preferred_element_type=jnp.float32
    )


def product_right(left_side, right_side):
    return lax.dot_general(
        left_side, right_side, (((1,), (1,)), ((), ())), preferred_element_type=jnp.float32
    )


def column_total(values):
    return jnp.sum(values.astype(jnp.float32), axis=0)


def normalize(values, gain_row, shift_row):
    centred = values - jnp.mean(values, axis=-1, keepdims=True)
    inv_scale = lax.rsqrt(jnp.mean(centred * centred, axis=-1, keepdims=True) + epsilon)
    normed = centred * inv_scale
    return (normed * gain_row + shift_row, normed, inv_scale)


def normalize_back(grad_out, normed, inv_scale, gain_row):
    grad_normed = grad_out * gain_row
    first_mean = jnp.mean(grad_normed, axis=-1, keepdims=True)
    second_mean = jnp.mean(grad_normed * normed, axis=-1, keepdims=True)
    grad_values = inv_scale * (grad_normed - first_mean - normed * second_mean)
    return (grad_values, jnp.sum(grad_out * normed, axis=0), jnp.sum(grad_out, axis=0))


def attention_scores(queries, keys_low, labels):
    heads_split = (queries.shape[0], HEADS, HEAD_DIM)
    scores = jnp.einsum(
        "qhd,khd->hqk",
        queries.reshape(heads_split),
        keys_low.reshape(heads_split),
        preferred_element_type=jnp.float32,
    ) * HEAD_DIM ** (-0.5)
    same_sentence = labels[:, None] == labels[None, :]
    return jnp.where(same_sentence[None], scores, -1000000000.0)


def layer_forward(hidden, weights, labels):
    (
        query_w,
        query_b,
        keys_w,
        value_w,
        value_b,
        mixer_w,
        mixer_b,
        gain_one,
        shift_one,
        expand_w,
        expand_b,
        shrink_w,
        shrink_b,
        gain_two,
        shift_two,
    ) = weights
    row_count = hidden.shape[0]
    queries = (product(hidden, query_w) + query_b).astype(jnp.bfloat16)
    keys_low = product(hidden, keys_w).astype(jnp.bfloat16)
    values = (product(hidden, value_w) + value_b).astype(jnp.bfloat16)
    scores = attention_scores(queries, keys_low, labels)
    row_peak = jnp.max(scores, axis=-1, keepdims=True)
    exponent = jnp.exp(scores - row_peak)
    totals = jnp.sum(exponent, axis=-1, keepdims=True)
    probs_low = (exponent / totals).astype(jnp.bfloat16)
    logsum = row_peak + jnp.log(totals)
    attended = jnp.einsum(
        "hqk,khd->qhd",
        probs_low,
        values.reshape(row_count, HEADS, HEAD_DIM),
        preferred_element_type=jnp.float32,
    )
    attended = attended.reshape(row_count, HEADS * HEAD_DIM).astype(jnp.bfloat16)
    mixed_out = product(attended, mixer_w) + mixer_b
    first_norm, normed_one, scale_one = normalize(
        hidden.astype(jnp.float32) + mixed_out, gain_one, shift_one
    )
    first_low = first_norm.astype(jnp.bfloat16)
    inner_act = product(first_low, expand_w) + expand_b
    normal_cdf = 0.5 * (1.0 + lax.erf(inner_act * root_half))
    gelu_slope = normal_cdf + inner_act * inv_root_tau * jnp.exp(-0.5 * inner_act * inner_act)
    active_low = (inner_act * normal_cdf).astype(jnp.bfloat16)
    outer_act = product(active_low, shrink_w) + shrink_b
    layer_final, normed_two, scale_two = normalize(first_norm + outer_act, gain_two, shift_two)
    kept_state = (
        queries,
        keys_low,
        values,
        logsum,
        attended,
        normed_one,
        scale_one,
        first_low,
        gelu_slope,
        active_low,
        normed_two,
        scale_two,
    )
    return (layer_final, kept_state)


def upper_backward(grad_final, weights, kept_state):
    (
        query_w,
        query_b,
        keys_w,
        value_w,
        value_b,
        mixer_w,
        mixer_b,
        gain_one,
        shift_one,
        expand_w,
        expand_b,
        shrink_w,
        shrink_b,
        gain_two,
        shift_two,
    ) = weights
    (
        queries,
        keys_low,
        values,
        logsum,
        attended,
        normed_one,
        scale_one,
        first_low,
        gelu_slope,
        active_low,
        normed_two,
        scale_two,
    ) = kept_state
    grad_two, dgain_two, dshift_two = normalize_back(grad_final, normed_two, scale_two, gain_two)
    outer_grad = grad_two.astype(jnp.bfloat16)
    inner_grad = (product_right(outer_grad, shrink_w) * gelu_slope).astype(jnp.bfloat16)
    grad_first = grad_two + product_right(inner_grad, expand_w)
    grad_one, dgain_one, dshift_one = normalize_back(grad_first, normed_one, scale_one, gain_one)
    mixed_grad = grad_one.astype(jnp.bfloat16)
    attended_grad = product_right(mixed_grad, mixer_w).astype(jnp.bfloat16)
    upper_terms = (
        product_left(attended, mixed_grad),
        column_total(mixed_grad),
        dgain_one,
        dshift_one,
        product_left(first_low, inner_grad),
        column_total(inner_grad),
        product_left(active_low, outer_grad),
        column_total(outer_grad),
        dgain_two,
        dshift_two,
    )
    return (grad_one, attended_grad, upper_terms)


def lower_backward(grad_one, attended_grad, hidden, weights, labels, kept_state):
    query_w = weights[0]
    keys_w = weights[2]
    value_w = weights[3]
    queries, keys_low, values, logsum = (kept_state[0], kept_state[1], kept_state[2], kept_state[3])
    row_count = hidden.shape[0]
    heads_split = (row_count, HEADS, HEAD_DIM)
    scores = attention_scores(queries, keys_low, labels)
    probability = jnp.exp(scores - logsum)
    grad_heads = attended_grad.reshape(heads_split)
    grad_probs = jnp.einsum(
        "qhd,khd->hqk", grad_heads, values.reshape(heads_split), preferred_element_type=jnp.float32
    )
    row_total = jnp.sum(probability * grad_probs, axis=-1, keepdims=True)
    score_grad = (probability * (grad_probs - row_total)).astype(jnp.bfloat16)
    query_grad = (
        (
            jnp.einsum(
                "hqk,khd->qhd",
                score_grad,
                keys_low.reshape(heads_split),
                preferred_element_type=jnp.float32,
            )
            * HEAD_DIM ** (-0.5)
        )
        .reshape(row_count, HEADS * HEAD_DIM)
        .astype(jnp.bfloat16)
    )
    keys_grad = (
        (
            jnp.einsum(
                "hqk,qhd->khd",
                score_grad,
                queries.reshape(heads_split),
                preferred_element_type=jnp.float32,
            )
            * HEAD_DIM ** (-0.5)
        )
        .reshape(row_count, HEADS * HEAD_DIM)
        .astype(jnp.bfloat16)
    )
    value_grad = (
        jnp.einsum(
            "hqk,qhd->khd",
            probability.astype(jnp.bfloat16),
            grad_heads,
            preferred_element_type=jnp.float32,
        )
        .reshape(row_count, HEADS * HEAD_DIM)
        .astype(jnp.bfloat16)
    )
    grad_hidden = (
        grad_one
        + product_right(query_grad, query_w)
        + product_right(keys_grad, keys_w)
        + product_right(value_grad, value_w)
    )
    lower_terms = (
        product_left(hidden, query_grad),
        column_total(query_grad),
        product_left(hidden, keys_grad),
        product_left(hidden, value_grad),
        column_total(value_grad),
    )
    return (grad_hidden, lower_terms)


def body(
    tokens,
    cotangent,
    sentence_ids,
    query_weight,
    query_bias,
    keys_weight,
    value_weight,
    value_bias,
    mixer_weight,
    mixer_bias,
    first_gain,
    first_shift,
    expand_weight,
    expand_bias,
    shrink_weight,
    shrink_bias,
    second_gain,
    second_shift,
):
    section_index = lax.axis_index("section")
    weights = tuple(
        (
            stored[0]
            for stored in (
                query_weight,
                query_bias,
                keys_weight,
                value_weight,
                value_bias,
                mixer_weight,
                mixer_bias,
                first_gain,
                first_shift,
                expand_weight,
                expand_bias,
                shrink_weight,
                shrink_bias,
                second_gain,
                second_shift,
            )
        )
    )
    row_count = ROWS
    micro_count = tokens.shape[0] // row_count
    features = tokens.shape[1]
    token_blocks = tokens.reshape(micro_count, row_count, features)
    grad_blocks = cotangent.reshape(micro_count, row_count, features)
    label_blocks = sentence_ids.reshape(micro_count, row_count)
    received = jnp.zeros((row_count, features), jnp.bfloat16)
    inputs_kept = []
    outputs_kept = []
    states_kept = []
    for forward_tick in range(micro_count + 1):
        block_index = jnp.clip(forward_tick - section_index, 0, micro_count - 1)
        labels = lax.dynamic_index_in_dim(label_blocks, block_index, 0, keepdims=False)
        hidden = jnp.where(
            section_index == 0, token_blocks[min(forward_tick, micro_count - 1)], received
        )
        layer_final, kept_state = layer_forward(hidden, weights, labels)
        final_low = layer_final.astype(jnp.bfloat16)
        inputs_kept.append(hidden)
        outputs_kept.append(final_low)
        states_kept.append(kept_state)
        if forward_tick < micro_count:
            received = passed_along(final_low, "section", 1)
    input_stack = jnp.stack(inputs_kept)
    back_received = jnp.zeros((row_count, features), jnp.bfloat16)
    running = tuple((jnp.zeros(stored.shape, jnp.float32) for stored in weights))
    grads_kept = []
    for backward_tick in range(micro_count + 1):
        block_index = backward_tick - 1 + section_index
        valid_factor = ((block_index >= 0) & (block_index < micro_count)).astype(jnp.float32)
        clipped = jnp.clip(block_index, 0, micro_count - 1)
        tick_slot = jnp.clip(block_index + section_index, 0, micro_count)
        labels = lax.dynamic_index_in_dim(label_blocks, clipped, 0, keepdims=False)
        hidden = lax.dynamic_index_in_dim(input_stack, tick_slot, 0, keepdims=False)
        kept_state = layer_forward(hidden, weights, labels)[1]
        grad_final = jnp.where(
            section_index == 1, grad_blocks[min(backward_tick, micro_count - 1)], back_received
        ).astype(jnp.float32)
        grad_one, attended_grad, upper_terms = upper_backward(grad_final, weights, kept_state)
        upper_sums = tuple(
            (current + valid_factor * addend for current, addend in zip(running[5:], upper_terms))
        )
        grad_hidden, lower_terms = lower_backward(
            grad_one, attended_grad, hidden, weights, labels, kept_state
        )
        lower_sums = tuple(
            (current + valid_factor * addend for current, addend in zip(running[:5], lower_terms))
        )
        running = tuple(lower_sums) + tuple(upper_sums)
        grad_low = grad_hidden.astype(jnp.bfloat16)
        grads_kept.append(grad_low)
        if backward_tick < micro_count:
            back_received = passed_along(grad_low, "section", -1)
    summed = tuple(lax.psum(running, "batch"))
    layer_out = lax.dynamic_slice_in_dim(
        jnp.stack(outputs_kept), section_index, micro_count, 0
    ).reshape(1, micro_count * row_count, features)
    layer_in_grad = lax.dynamic_slice_in_dim(
        jnp.stack(grads_kept), 1 - section_index, micro_count, 0
    ).reshape(1, micro_count * row_count, features)
    return (layer_out, layer_in_grad) + tuple((total[None] for total in summed))


def solution(mesh):
    placed = (
        P("batch", None),
        P("batch", None),
        P("batch"),
        P("section", None, None),
        P("section", None),
        P("section", None, None),
        P("section", None, None),
        P("section", None),
        P("section", None, None),
        P("section", None),
        P("section", None),
        P("section", None),
        P("section", None, None),
        P("section", None),
        P("section", None, None),
        P("section", None),
        P("section", None),
        P("section", None),
    )
    return jax.shard_map(
        body,
        mesh=mesh,
        in_specs=placed,
        out_specs=(
            P("section", "batch", None),
            P("section", "batch", None),
            P("section", None, None),
            P("section", None),
            P("section", None, None),
            P("section", None, None),
            P("section", None),
            P("section", None, None),
            P("section", None),
            P("section", None),
            P("section", None),
            P("section", None, None),
            P("section", None),
            P("section", None, None),
            P("section", None),
            P("section", None),
            P("section", None),
        ),
        check_vma=False,
    )
```

profile of v0, /device:TPU:0, one launch (start us, length us, event | category | flops | bytes accessed | tf_op | source)
XLA Modules:
  0.0 1291.4 jit_solution(11723213610830494410)
XLA Ops:
  25.4 8.6 fusion.334
  34.0 5.9 fusion.141
  67.0 11.0 fusion.337
  78.0 5.8 fusion.140
  141.4 7.0 fusion.76
  170.3 12.3 multiply_convert_fusion.4
  182.6 6.3 fusion.345
  208.3 9.6 convert_reduce_fusion.14
  217.9 9.7 multiply_reduce_fusion.2
  227.6 7.2 multiply_convert_fusion.2
  300.1 7.9 fusion.341
  317.0 11.2 fusion.346
  328.2 6.0 fusion.139
  373.5 9.6 convert_reduce_fusion.13
  383.2 9.7 multiply_reduce_fusion.1
  392.9 7.5 multiply_convert_fusion.1
  448.3 9.6 convert_reduce_fusion.12
  458.0 9.8 multiply_reduce_fusion
  467.8 7.1 multiply_convert_fusion
  480.4 13.1 %add_bitcast_fusion = f32[1,3072,768]{2,1,0:T(8,128)} fusion(f32[3072,768]{1,0:T(8,128)} %fusion.293, f32[3072,768]{1,0:T(8,128)} %fusion.299, f32[]{:T(128)S(6)} %convert_element_type.539, f32[]{:T(128)S(6)} %convert_element_type.538, f32[]{:T(128)S(6)} %convert_element_type.537, f32[512,768]{1,0:T(8,128)} %copy-done.46, f32[512,3072]{1,0:T(8,128)} %copy-done.47, ...), kind=kOutput, calls=%fused_computation.42 | convolution fusion | flops 2437545984 | bytes 36188172 | tf_op jit(solution)/shard_map/dot_general | solution.py:27
  494.2 10.3 add_bitcast_fusion.1
  528.2 83.6 %all-reduce = (f32[1,768]{1,0:T(1,128)}, f32[1,768]{1,0:T(1,128)}, f32[1,768]{1,0:T(1,128)}, f32[1,768]{1,0:T(1,128)}, f32[1,768]{1,0:T(1,128)}, /*index=5*/f32[...) all-reduce(f32[1,768]{1,0:T(1,128)} %broadcast_in_dim.92, ...), channel_id=1, replica_groups=mesh['section'=2,'batch'=16] {'batch'}, use_global_device_ids=true, to_apply=%region_55.56 | all-reduce | flops 9216 | bytes 73728 | tf_op jit(solution)/shard_map/psum | solution.py:349
  621.2 640.0 %all-reduce.4.cloned.1.call-done = (f32[1,768,768]{2,1,0:T(8,128)}, f32[1,768,768]{2,1,0:T(8,128)}, f32[1,768,768]{2,1,0:T(8,128)}, f32[1,768,768]{2,1,0:T(8,128...) async-done(((f32[1,768,768]{2,1,0:T(8,128)}, f32[1,768,768]{2,1,0:T(8,128)}, f32[1,768,768]{2,1,0:T(8,128)}, f32[1,768,768]{2,1,0:T(8,128)}, f32[1,768,3072]{2,1,0:T(8,128)}, ...) | async-done | bytes 28311568 | tf_op jit(solution)/shard_map/psum | solution.py:349
  1271.0 9.3 copy.144
  (741 shorter events, 356.2 us)
Async XLA Ops:
  7.2 32.7 %copy-start = (bf16[1,768,768]{2,1,0:T(8,128)(2,1)S(1)}, bf16[1,768,768]{2,1,0:T(8,128)(2,1)}, u32[]{:S(2)}) copy-start(bf16[1,768,768]{2,1,0:T(8,128)(2,1)} %param.26) | copy-start | bytes 3538948
  7.2 1254.0 %all-reduce.4.cloned.1.call-start = ((), (), s32[]{:S(2)}) async-start(), calls=%async_computation | async-start | bytes 56623104 | tf_op jit(solution)/shard_map/psum | solution.py:349
  53.4 138.3 %copy-start.103 = (f32[768]{0:T(1024)}, f32[768]{0:T(1024)S(1)}, u32[]{:S(2)}) copy-start(f32[768]{0:T(1024)S(1)} %reduce.12) | copy-start | bytes 9220
  53.4 42.5 %copy-start.110 = (f32[768]{0:T(1024)}, f32[768]{0:T(1024)S(1)}, u32[]{:S(2)}) copy-start(f32[768]{0:T(1024)S(1)} %reduce.13) | copy-start | bytes 9220
  53.8 4.4 collective-permute-start
  58.3 25.4 %copy-start.81 = (bf16[512,768]{1,0:T(8,128)(2,1)}, bf16[512,768]{1,0:T(8,128)(2,1)S(1)}, u32[]{:S(2)}) copy-start(bf16[512,768]{1,0:T(8,128)(2,1)S(1)} %broadcast_select_fusion.3) | copy-start | bytes 2359300
  98.1 7.9 collective-permute-start.1
  139.7 42.9 %copy-start.131 = (f32[512]{0:T(512)}, f32[512]{0:T(512)S(1)}, u32[]{:S(2)}) copy-start(f32[512]{0:T(512)S(1)} %broadcast_multiply_fusion.17) | copy-start | bytes 6148
  169.5 99.1 %copy-start.126 = (f32[512]{0:T(512)}, f32[512]{0:T(512)S(1)}, u32[]{:S(2)}) copy-start(f32[512]{0:T(512)S(1)} %broadcast_multiply_fusion.11) | copy-start | bytes 6148
  170.2 22.6 %slice-start.17 = ((s8[4718592]{0:T(1024)(128)(4,1)}), s8[4194304]{0:T(1024)(128)(4,1)S(1)}, s32[]{:S(2)}) async-start(s8[4718592]{0:T(1024)(128)(4,1)} %bitcast.507), calls=%async_computation.18 | async-start | bytes 8388608
  170.2 22.6 %slice-start.31 = ((s8[6291456]{0:T(1024)(128)(4,1)}), s8[4194304]{0:T(1024)(128)(4,1)S(1)}, s32[]{:S(2)}) async-start(s8[6291456]{0:T(1024)(128)(4,1)} %bitcast.524), calls=%async_computation.32 | async-start | bytes 8388608
  208.2 19.3 %slice-start.6 = ((s8[12582912]{0:T(1024)(128)(4,1)}), s8[4194304]{0:T(1024)(128)(4,1)S(1)}, s32[]{:S(2)}) async-start(s8[12582912]{0:T(1024)(128)(4,1)} %bitcast.421), calls=%async_computation.7 | async-start | bytes 8388608
  208.2 19.3 %slice-start.7 = ((s8[12582912]{0:T(1024)(128)(4,1)}), s8[4194304]{0:T(1024)(128)(4,1)S(1)}, s32[]{:S(2)}) async-start(s8[12582912]{0:T(1024)(128)(4,1)} %bitcast.421), calls=%async_computation.8 | async-start | bytes 8388608
  267.1 87.1 %collective-permute-start.2 = (bf16[512,768]{1,0:T(8,128)(2,1)}, bf16[512,768]{1,0:T(8,128)(2,1)}, u32[]{:S(2)}, u32[]{:S(2)}) collective-permute-start(bf16[512,768]{1,0:T(8,128)(2,1)} %add_convert_fusion.6), channel_id=1, source_target_pairs={{16,0},{17,1},{18,2},{19,3},{20,4},{21,5},{22,6},{23,7},{24,8},{25... | collective-permute-start | bytes 2359304 | tf_op jit(solution)/shard_map/ppermute | solution.py:19
  336.0 22.1 %slice-start.21 = ((s8[4718592]{0:T(1024)(128)(4,1)}), s8[4194304]{0:T(1024)(128)(4,1)S(1)}, s32[]{:S(2)}) async-start(s8[4718592]{0:T(1024)(128)(4,1)} %bitcast.511), calls=%async_computation.22 | async-start | bytes 8388608
  336.0 22.1 %slice-start.33 = ((s8[6291456]{0:T(1024)(128)(4,1)}), s8[4194304]{0:T(1024)(128)(4,1)S(1)}, s32[]{:S(2)}) async-start(s8[6291456]{0:T(1024)(128)(4,1)} %bitcast.526), calls=%async_computation.34 | async-start | bytes 8388608
  341.3 16.8 %slice-start.22 = ((s8[4718592]{0:T(1024)(128)(4,1)}), s8[524288]{0:T(1024)(128)(4,1)S(1)}, s32[]{:S(2)}) async-start(s8[4718592]{0:T(1024)(128)(4,1)} %bitcast.511), calls=%async_computation.23 | async-start | bytes 1048576
  341.3 16.7 %slice-start.34 = ((s8[6291456]{0:T(1024)(128)(4,1)}), s8[2097152]{0:T(1024)(128)(4,1)S(1)}, s32[]{:S(2)}) async-start(s8[6291456]{0:T(1024)(128)(4,1)} %bitcast.526), calls=%async_computation.35 | async-start | bytes 4194304
  373.5 19.3 %slice-start = ((s8[12582912]{0:T(1024)(128)(4,1)}), s8[4194304]{0:T(1024)(128)(4,1)S(1)}, s32[]{:S(2)}) async-start(s8[12582912]{0:T(1024)(128)(4,1)} %bitcast.417), calls=%async_computation.1 | async-start | bytes 8388608
  373.5 19.3 %slice-start.1 = ((s8[12582912]{0:T(1024)(128)(4,1)}), s8[4194304]{0:T(1024)(128)(4,1)S(1)}, s32[]{:S(2)}) async-start(s8[12582912]{0:T(1024)(128)(4,1)} %bitcast.417), calls=%async_computation.2 | async-start | bytes 8388608
  419.2 9.6 collective-permute-start.3
  448.3 19.5 %slice-start.3 = ((s8[12582912]{0:T(1024)(128)(4,1)}), s8[4194304]{0:T(1024)(128)(4,1)S(1)}, s32[]{:S(2)}) async-start(s8[12582912]{0:T(1024)(128)(4,1)} %bitcast.419), calls=%async_computation.4 | async-start | bytes 8388608
  448.3 19.5 %slice-start.4 = ((s8[12582912]{0:T(1024)(128)(4,1)}), s8[4194304]{0:T(1024)(128)(4,1)S(1)}, s32[]{:S(2)}) async-start(s8[12582912]{0:T(1024)(128)(4,1)} %bitcast.419), calls=%async_computation.5 | async-start | bytes 8388608
  521.1 90.7 %copy-start.45 = (bf16[12,64,512]{2,1,0:T(8,128)(2,1)S(1)}, bf16[12,64,512]{2,1,0:T(8,128)(2,1)}, u32[]{:S(2)}) copy-start(bf16[12,64,512]{2,1,0:T(8,128)(2,1)} %get-tuple-element.128) | copy-start | bytes 2359300
  (236 other events, 1059.5 us)
Sparse Core Ops, SparseCore 0:
  518.3 742.8 all-reduce.3
where the time goes:
time: 1300 us; the launch traced here: 1290 us
  waiting for transfers between devices  641 us (49%)
  matrix products  372 us (29%)
  local copies, waits for them, and re-layouts  97.2 us (7%)
  blocking collectives  83.6 us (6%)
  other arithmetic  71.9 us (6%)
  between operations  17.1 us (1%)
    psum x1, waiting for transfers between devices, body(): summed = tuple(lax.psum(running, 'batch'))  640 us
    dot_general x36, matrix products, product(): return jnp.dot(left_side, right_side, preferred_element_type=jnp.float32)  111 us
    psum x1, blocking collectives, body(): summed = tuple(lax.psum(running, 'batch'))  83.6 us
    dot_general x18, matrix products, product_left(): lax.dot_general(left_side, right_side, (((0,), (0,)), ((), ())), preferre...  74.1 us
    unnamed x516, local copies, waits for them, and re-layouts  47.5 us
    dot_general x18, matrix products, product_right(): lax.dot_general(left_side, right_side, (((1,), (1,)), ((), ())), preferre...  42.2 us
    dot_general x6, matrix products, layer_forward(): jnp.einsum('hqk,khd->qhd', probs_low, values.reshape(row_count, HEADS, HE...  32.4 us
    sub x3, matrix products, layer_forward(): exponent = jnp.exp(scores - row_peak)  30.8 us
  transfers between devices with their start and end apart: 5, of which 2 were waited for; matrix products, arithmetic and copies ran while one was open for 9% of the time, Pallas kernels for 0%

commit v1 on v0

--- a/solution.py
+++ b/solution.py
@@ -1,6 +1,10 @@
+import functools
+
 import jax
 import jax.numpy as jnp
 from jax import lax
+from jax.experimental import pallas as pl
+from jax.experimental.pallas import tpu as pltpu
 from jax.sharding import PartitionSpec as P
 
 HEADS = 12
@@ -13,10 +17,305 @@
 inv_root_tau = 0.3989422804014327
 
 
-def passed_along(shard, axis, by):
-    length = lax.axis_size(axis)
-    pairs = [(i, i + by) for i in range(length) if 0 <= i + by < length]
-    return lax.ppermute(shard, axis, pairs)
+MESH = pl.DeviceIdType.MESH
+NB = 12
+BLK = 768
+COL = 384
+HALF = 384
+CH = 96
+SUB = 48
+NSTAGE = 12
+
+
+def when(cond, fn):
+    if isinstance(cond, bool):
+        if cond:
+            fn()
+    else:
+        pl.when(cond)(fn)
+
+
+def coords():
+    s = lax.axis_index("section")
+    b = lax.axis_index("batch")
+    return s, b // 4, (b // 2) % 2, b % 2
+
+
+def dev(s, z, y, x):
+    return (s, z * 4 + y * 2 + x)
+
+
+class Comm:
+    def __init__(self, refs):
+        self.__dict__.update(refs)
+        s, z, y, x = coords()
+        self.s, self.p = s, z
+        self.core = dev(1 - s, z, y, x)
+        xn, yn = dev(s, z, y, 1 - x), dev(s, z, 1 - y, x)
+        self.u = (x, y)
+        self.w = (y, x)
+        self.n1 = (xn, yn)
+        self.n3 = (yn, xn)
+        self.up = dev(s, jnp.minimum(z + 1, 3), y, x)
+        self.dn = dev(s, jnp.maximum(z - 1, 0), y, x)
+
+    def barrier(self):
+        s, z, y, x = coords()
+        bar = pltpu.get_barrier_semaphore()
+        peers = [self.core, self.n1[0], self.n1[1]] + [dev(s, lax.rem(z + k, 4), y, x) for k in (1, 2, 3)]
+        for d in peers:
+            pl.semaphore_signal(bar, inc=1, device_id=d, device_id_type=MESH)
+        pl.semaphore_wait(bar, len(peers))
+
+    def remote(self, src, dst, ss, rs, d):
+        return pltpu.make_async_remote_copy(src_ref=src, dst_ref=dst, send_sem=ss, recv_sem=rs, device_id=d, device_id_type=MESH)
+
+    def prt_copy(self, src, b):
+        return self.remote(src, self.prt.at[b], self.prt_s.at[b], self.prt_r.at[b], self.core)
+
+    def loads(self, st, b):
+        sl = lax.rem(b, 2)
+        cols = pl.ds(st * COL, COL)
+        return (
+            pltpu.make_async_copy(self.acc.at[b, :, cols], self.lda.at[st, sl], self.ld_sem.at[st, sl, 0]),
+            pltpu.make_async_copy(self.prt.at[b, :, cols], self.ldp.at[st, sl], self.ld_sem.at[st, sl, 1]),
+        )
+
+    def s0(self, b):
+        self.prt_copy(self.prt.at[b], b).wait_recv()
+        for st in (0, 1):
+            for c in self.loads(st, b):
+                c.start()
+
+    def r1_copy(self, st, b):
+        sl = lax.rem(b, 2)
+        rows = pl.ds(pl.multiple_of((1 - self.u[st]) * HALF, HALF), HALF)
+        return self.remote(self.lda.at[st, sl, rows], self.r1.at[st, sl], self.r1_s.at[st, sl], self.r1_r.at[st, sl], self.n1[st])
+
+    def s1(self, b):
+        sl = lax.rem(b, 2)
+        for st in (0, 1):
+            for c in self.loads(st, b):
+                c.wait()
+            oth = pl.ds(pl.multiple_of((1 - self.u[st]) * HALF, HALF), HALF)
+            own = pl.ds(pl.multiple_of(self.u[st] * HALF, HALF), HALF)
+            self.lda[st, sl, oth] += self.ldp[st, sl, oth]
+            self.r1_copy(st, b).start()
+            self.lda[st, sl, own] += self.ldp[st, sl, own]
+
+    def zsend(self, st, b, lo, hi, up):
+        zs = lax.rem(b, 4)
+        if up:
+            return self.remote(self.zbuf.at[st, zs, pl.ds(lo, hi - lo)], self.ru.at[st, zs, pl.ds(lo - CH, hi - lo)],
+                               self.ru_s.at[st, zs], self.ru_r.at[st, zs], self.up)
+        return self.remote(self.zbuf.at[st, zs, pl.ds(lo, hi - lo)], self.rd.at[st, zs, pl.ds(lo, hi - lo)],
+                           self.rd_s.at[st, zs], self.rd_r.at[st, zs], self.dn)
+
+    def zadd(self, st, b, lo, hi, up):
+        zs = lax.rem(b, 4)
+        self.zsend(st, b, lo, hi, up).wait_recv()
+        if up:
+            self.zbuf[st, zs, lo:hi] += self.ru[st, zs, lo - CH:hi - CH]
+        else:
+            self.zbuf[st, zs, lo:hi] += self.rd[st, zs, lo:hi]
+
+    def s2(self, b):
+        sl, zs = lax.rem(b, 2), lax.rem(b, 4)
+        for st in (0, 1):
+            self.r1_copy(st, b).wait()
+            own = pl.ds(pl.multiple_of(self.u[st] * HALF, HALF), HALF)
+            self.zbuf[st, zs] = self.lda[st, sl, own] + self.r1[st, sl]
+            pl.when(self.p == 0)(lambda: self.zsend(st, b, CH, 4 * CH, True).start())
+            pl.when(self.p == 3)(lambda: self.zsend(st, b, 0, 3 * CH, False).start())
+
+    def s3(self, b):
+        for st in (0, 1):
+            @pl.when(self.p == 1)
+            def _():
+                self.zadd(st, b, CH, 4 * CH, True)
+                self.zsend(st, b, 2 * CH, 4 * CH, True).start()
+
+            @pl.when(self.p == 2)
+            def _():
+                self.zadd(st, b, 0, 3 * CH, False)
+                self.zsend(st, b, 0, 2 * CH, False).start()
+
+    def s4(self, b):
+        for st in (0, 1):
+            @pl.when(self.p == 2)
+            def _():
+                self.zadd(st, b, 2 * CH, 4 * CH, True)
+                self.zsend(st, b, 3 * CH, 4 * CH, True).start()
+
+            @pl.when(self.p == 1)
+            def _():
+                self.zadd(st, b, 0, 2 * CH, False)
+                self.zsend(st, b, 0, CH, False).start()
+
+    def r3_copy(self, st, b):
+        sl, zs = lax.rem(b, 2), lax.rem(b, 4)
+        rows = pl.ds(pl.multiple_of(self.p * CH + (1 - self.w[st]) * SUB, SUB), SUB)
+        return self.remote(self.zbuf.at[st, zs, rows], self.r3.at[st, sl], self.r3_s.at[st, sl], self.r3_r.at[st, sl], self.n3[st])
+
+    def s5(self, b):
+        for st in (0, 1):
+            pl.when(self.p == 0)(lambda: self.zadd(st, b, 0, CH, False))
+            pl.when(self.p == 3)(lambda: self.zadd(st, b, 3 * CH, 4 * CH, True))
+            self.r3_copy(st, b).start()
+
+    def res_at(self, st, b, c, lo, n, u):
+        rows = pl.ds(pl.multiple_of(u * HALF + c * CH + lo, SUB), n)
+        return self.res.at[b, rows, pl.ds(st * COL, COL)]
+
+    def fin_copies(self, st, b):
+        sl = lax.rem(b, 2)
+        there = self.res_at(st, b, self.p, self.w[st] * SUB, SUB, self.u[st])
+        return (
+            self.remote(self.fin.at[st, sl], there, self.ag_s.at[st, 3, 0, lax.rem(b, 4)], self.wr.at[st, b], self.n3[st]),
+            pltpu.make_async_copy(self.fin.at[st, sl], there, self.ag_s.at[st, 3, 1, lax.rem(b, 4)]),
+        )
+
+    def s6(self, b):
+        sl, zs = lax.rem(b, 2), lax.rem(b, 4)
+        for st in (0, 1):
+            self.r3_copy(st, b).wait()
+            pl.when(self.p == 0)(lambda: self.zsend(st, b, CH, 4 * CH, True).wait_send())
+            pl.when(self.p == 3)(lambda: self.zsend(st, b, 0, 3 * CH, False).wait_send())
+
+            @pl.when(self.p == 1)
+            def _():
+                self.zsend(st, b, 2 * CH, 4 * CH, True).wait_send()
+                self.zsend(st, b, 0, CH, False).wait_send()
+
+            @pl.when(self.p == 2)
+            def _():
+                self.zsend(st, b, 0, 2 * CH, False).wait_send()
+                self.zsend(st, b, 3 * CH, 4 * CH, True).wait_send()
+
+            rows = pl.ds(pl.multiple_of(self.p * CH + self.w[st] * SUB, SUB), SUB)
+            self.fin[st, sl] = self.zbuf[st, zs, rows] + self.r3[st, sl]
+            for c in self.fin_copies(st, b):
+                c.start()
+
+    def ag(self, st, b, c, d):
+        here = self.res_at(st, b, c, 0, CH, self.u[st])
+        to, sem = ((self.up, self.zr), (self.dn, self.zr), (self.n1[st], self.xr))[d]
+        return self.remote(here, here, self.ag_s.at[st, d, c, lax.rem(b, 4)], sem.at[st, b, c], to)
+
+    def spread(self, st, b, c, up, down):
+        if up:
+            pl.when(self.p < 3)(lambda: self.ag(st, b, c, 0).start())
+        if down:
+            pl.when(self.p > 0)(lambda: self.ag(st, b, c, 1).start())
+        self.ag(st, b, c, 2).start()
+
+    def s7(self, b):
+        for st in (0, 1):
+            far, near = self.fin_copies(st, b)
+            far.wait()
+            near.wait()
+            self.spread(st, b, self.p, True, True)
+
+    def hop(self, k, b):
+        for st in (0, 1):
+            @pl.when(self.p >= k)
+            def _():
+                self.ag(st, b, self.p - k, 0).wait_recv()
+                self.spread(st, b, self.p - k, True, False)
+
+            @pl.when(self.p <= 3 - k)
+            def _():
+                self.ag(st, b, self.p + k, 1).wait_recv()
+                self.spread(st, b, self.p + k, False, True)
+
+    def s8(self, b):
+        self.hop(1, b)
+
+    def s9(self, b):
+        self.hop(2, b)
+
+    def s10(self, b):
+        self.hop(3, b)
+
+    def s11(self, b):
+        for st in (0, 1):
+            for c in range(4):
+                got = self.ag(st, b, c, 2)
+                got.wait_send()
+                got.wait_recv()
+                pl.when((self.p < 3) & (self.p >= c))(lambda: self.ag(st, b, c, 0).wait_send())
+                pl.when((self.p > 0) & (self.p <= c))(lambda: self.ag(st, b, c, 1).wait_send())
+
+    def tick(self, t):
+        stages = (self.s0, self.s1, self.s2, self.s3, self.s4, self.s5, self.s6, self.s7, self.s8, self.s9, self.s10, self.s11)
+        for k in reversed(range(NSTAGE)):
+            b = t - k
+            when((b >= 0) & (b < NB), lambda: stages[k](b))
+
+    def vec_copy(self, k):
+        s, z, y, x = coords()
+        to = (self.core, dev(s, z, y, 1 - x), dev(s, z, 1 - y, x), dev(s, z + 1 - 2 * lax.rem(z, 2), y, x), dev(s, lax.rem(z + 2, 4), y, x))[k]
+        src = self.vec.at[1 - s] if k == 0 else self.vcur.at[k - 1]
+        return self.remote(src, self.vrecv.at[k], self.v_s.at[k], self.v_r.at[k], to)
+
+    def vec_step(self, k):
+        self.vec_copy(k).wait()
+        s = self.s
+        before = self.vec[s] if k == 0 else self.vcur[k - 1]
+        self.vcur[k] = before + self.vrecv[k]
+        if k < 4:
+            self.vec_copy(k + 1).start()
+
+
+def scratch():
+    bf = jnp.bfloat16
+    dma = pltpu.SemaphoreType.DMA
+    return dict(
+        lda=pltpu.VMEM((2, 2, BLK, COL), bf), ldp=pltpu.VMEM((2, 2, BLK, COL), bf),
+        r1=pltpu.VMEM((2, 2, HALF, COL), bf), zbuf=pltpu.VMEM((2, 4, HALF, COL), bf),
+        ru=pltpu.VMEM((2, 4, 3 * CH, COL), bf), rd=pltpu.VMEM((2, 4, 3 * CH, COL), bf),
+        r3=pltpu.VMEM((2, 2, SUB, COL), bf), fin=pltpu.VMEM((2, 2, SUB, COL), bf),
+        vcur=pltpu.VMEM((5, 16, BLK), jnp.float32), vrecv=pltpu.VMEM((5, 16, BLK), jnp.float32),
+        prt_s=dma((NB,)), prt_r=dma((NB,)), ld_sem=dma((2, 2, 2)), r1_s=dma((2, 2)), r1_r=dma((2, 2)),
+        ru_s=dma((2, 4)), ru_r=dma((2, 4)), rd_s=dma((2, 4)), rd_r=dma((2, 4)), r3_s=dma((2, 2)), r3_r=dma((2, 2)),
+        ag_s=dma((2, 4, 4, 4)), wr=dma((2, NB)), zr=dma((2, NB, 4)), xr=dma((2, NB, 4)), v_s=dma((5,)), v_r=dma((5,)),
+    )
+
+
+def reduce_kernel(names, grads, vec, res, out_vec, prt, *rest):
+    refs = dict(zip(names, rest))
+    s = lax.axis_index("section")
+    c = Comm(dict(refs, acc=grads.at[s], prt=prt, res=res, vec=vec))
+    c.barrier()
+    for b in range(NB):
+        c.prt_copy(grads.at[1 - s, b], b).start()
+    c.vec_copy(0).start()
+
+    def step(t, carry):
+        c.tick(t)
+        return carry
+
+    lax.fori_loop(0, NB + NSTAGE - 1, step, 0)
+    for k in range(5):
+        c.vec_step(k)
+    for b in range(NB):
+        c.prt_copy(grads.at[1 - s, b], b).wait_send()
+    out_vec[...] = c.vcur[4]
+
+
+def reduce_grads(grads, vec):
+    sc = scratch()
+    hbm = pl.BlockSpec(memory_space=pl.ANY)
+    vm = pl.BlockSpec(memory_space=pltpu.VMEM)
+    blocks = jax.ShapeDtypeStruct((NB, BLK, BLK), jnp.bfloat16)
+    res, out_vec, _ = pl.pallas_call(
+        functools.partial(reduce_kernel, tuple(sc)),
+        out_shape=(blocks, jax.ShapeDtypeStruct((16, BLK), jnp.float32), blocks),
+        in_specs=[hbm, vm], out_specs=(hbm, vm, hbm),
+        scratch_shapes=list(sc.values()),
+        compiler_params=pltpu.CompilerParams(collective_id=0, has_side_effects=True, vmem_limit_bytes=48 * 2**20),
+    )(grads, vec)
+    return res, out_vec
 
 
 def product(left_side, right_side):
@@ -250,110 +549,67 @@
     return (grad_hidden, lower_terms)
 
 
-def body(
-    tokens,
-    cotangent,
-    sentence_ids,
-    query_weight,
-    query_bias,
-    keys_weight,
-    value_weight,
-    value_bias,
-    mixer_weight,
-    mixer_bias,
-    first_gain,
-    first_shift,
-    expand_weight,
-    expand_bias,
-    shrink_weight,
-    shrink_bias,
-    second_gain,
-    second_shift,
-):
-    section_index = lax.axis_index("section")
-    weights = tuple(
-        (
-            stored[0]
-            for stored in (
-                query_weight,
-                query_bias,
-                keys_weight,
-                value_weight,
-                value_bias,
-                mixer_weight,
-                mixer_bias,
-                first_gain,
-                first_shift,
-                expand_weight,
-                expand_bias,
-                shrink_weight,
-                shrink_bias,
-                second_gain,
-                second_shift,
-            )
-        )
-    )
-    row_count = ROWS
-    micro_count = tokens.shape[0] // row_count
-    features = tokens.shape[1]
-    token_blocks = tokens.reshape(micro_count, row_count, features)
-    grad_blocks = cotangent.reshape(micro_count, row_count, features)
-    label_blocks = sentence_ids.reshape(micro_count, row_count)
-    received = jnp.zeros((row_count, features), jnp.bfloat16)
-    inputs_kept = []
-    outputs_kept = []
-    states_kept = []
-    for forward_tick in range(micro_count + 1):
-        block_index = jnp.clip(forward_tick - section_index, 0, micro_count - 1)
-        labels = lax.dynamic_index_in_dim(label_blocks, block_index, 0, keepdims=False)
-        hidden = jnp.where(
-            section_index == 0, token_blocks[min(forward_tick, micro_count - 1)], received
-        )
-        layer_final, kept_state = layer_forward(hidden, weights, labels)
-        final_low = layer_final.astype(jnp.bfloat16)
-        inputs_kept.append(hidden)
-        outputs_kept.append(final_low)
-        states_kept.append(kept_state)
-        if forward_tick < micro_count:
-            received = passed_along(final_low, "section", 1)
-    input_stack = jnp.stack(inputs_kept)
-    back_received = jnp.zeros((row_count, features), jnp.bfloat16)
-    running = tuple((jnp.zeros(stored.shape, jnp.float32) for stored in weights))
-    grads_kept = []
-    for backward_tick in range(micro_count + 1):
-        block_index = backward_tick - 1 + section_index
-        valid_factor = ((block_index >= 0) & (block_index < micro_count)).astype(jnp.float32)
-        clipped = jnp.clip(block_index, 0, micro_count - 1)
-        tick_slot = jnp.clip(block_index + section_index, 0, micro_count)
-        labels = lax.dynamic_index_in_dim(label_blocks, clipped, 0, keepdims=False)
-        hidden = lax.dynamic_index_in_dim(input_stack, tick_slot, 0, keepdims=False)
-        kept_state = layer_forward(hidden, weights, labels)[1]
-        grad_final = jnp.where(
-            section_index == 1, grad_blocks[min(backward_tick, micro_count - 1)], back_received
-        ).astype(jnp.float32)
-        grad_one, attended_grad, upper_terms = upper_backward(grad_final, weights, kept_state)
-        upper_sums = tuple(
-            (current + valid_factor * addend for current, addend in zip(running[5:], upper_terms))
-        )
-        grad_hidden, lower_terms = lower_backward(
-            grad_one, attended_grad, hidden, weights, labels, kept_state
-        )
-        lower_sums = tuple(
-            (current + valid_factor * addend for current, addend in zip(running[:5], lower_terms))
-        )
-        running = tuple(lower_sums) + tuple(upper_sums)
-        grad_low = grad_hidden.astype(jnp.bfloat16)
-        grads_kept.append(grad_low)
-        if backward_tick < micro_count:
-            back_received = passed_along(grad_low, "section", -1)
-    summed = tuple(lax.psum(running, "batch"))
-    layer_out = lax.dynamic_slice_in_dim(
-        jnp.stack(outputs_kept), section_index, micro_count, 0
-    ).reshape(1, micro_count * row_count, features)
-    layer_in_grad = lax.dynamic_slice_in_dim(
-        jnp.stack(grads_kept), 1 - section_index, micro_count, 0
-    ).reshape(1, micro_count * row_count, features)
-    return (layer_out, layer_in_grad) + tuple((total[None] for total in summed))
+def grads_blocks(lower, upper):
+    q_dw, q_db, k_dw, v_dw, v_db = lower
+    m_dw, m_db, g1, s1, e_dw, e_db, sh_dw, sh_db, g2, s2 = upper
+    low = lambda a: a.astype(jnp.bfloat16)
+    blocks = jnp.concatenate([
+        low(sh_dw).reshape(4, BLK, BLK),
+        low(e_dw).reshape(BLK, 4, BLK).transpose(1, 0, 2),
+        jnp.stack([low(m_dw), low(q_dw), low(k_dw), low(v_dw)]),
+    ])
+    rows = jnp.concatenate([
+        jnp.stack([q_db, v_db, m_db, g1, s1, sh_db, g2, s2]), e_db.reshape(4, BLK), jnp.zeros((4, BLK), jnp.float32)])
+    return blocks, rows
+
+
+def outputs_of(res, vec):
+    wide = lambda a: a.astype(jnp.float32)
+    sh_dw = wide(res[0:4].reshape(4 * BLK, BLK))
+    e_dw = wide(res[4:8].transpose(1, 0, 2).reshape(BLK, 4 * BLK))
+    m_dw, q_dw, k_dw, v_dw = (wide(res[i]) for i in (8, 9, 10, 11))
+    q_db, v_db, m_db, g1, s1, sh_db, g2, s2 = (vec[i] for i in range(8))
+    e_db = vec[8:12].reshape(4 * BLK)
+    return (q_dw, q_db, k_dw, v_dw, v_db, m_dw, m_db, g1, s1, e_dw, e_db, sh_dw, sh_db, g2, s2)
+
+
+def body(tokens, cotangent, sentence_ids, *stored):
+    s = lax.axis_index("section")
+    own = tuple(w[0] for w in stored)
+    other = tuple(lax.ppermute(w, "section", [(0, 1), (1, 0)]) for w in own)
+    first = tuple(jnp.where(s == 0, a, b) for a, b in zip(own, other))
+    second = tuple(jnp.where(s == 0, b, a) for a, b in zip(own, other))
+    half = tokens.shape[0] // 2
+    part = lambda a: lax.dynamic_slice_in_dim(a, s * half, half, 0)
+    micro = half // ROWS
+    h = part(tokens)
+    dy = part(cotangent)
+    labels = part(sentence_ids)
+    assert micro == 1
+    out0, kept0 = layer_forward(h, first, labels)
+    out0 = out0.astype(jnp.bfloat16)
+    out1, kept1 = layer_forward(out0, second, labels)
+    out1 = out1.astype(jnp.bfloat16)
+    go, ag, up1 = upper_backward(dy.astype(jnp.float32), second, kept1)
+    gh, lo1 = lower_backward(go, ag, out0, second, labels, kept1)
+    gin1 = gh.astype(jnp.bfloat16)
+    go, ag, up0 = upper_backward(gin1.astype(jnp.float32), first, kept0)
+    gh, lo0 = lower_backward(go, ag, h, first, labels, kept0)
+    gin0 = gh.astype(jnp.bfloat16)
+
+    def both(zero, one):
+        mine = jnp.where(s == 0, zero, one)
+        got = lax.ppermute(jnp.where(s == 0, one, zero), "section", [(0, 1), (1, 0)])
+        return jnp.concatenate([jnp.where(s == 0, mine, got), jnp.where(s == 0, got, mine)])[None]
+
+    if lax.axis_size("batch") == 16:
+        b0, v0 = grads_blocks(lo0, up0)
+        b1, v1 = grads_blocks(lo1, up1)
+        sums = outputs_of(*reduce_grads(jnp.stack([b0, b1]), jnp.stack([v0, v1])))
+    else:
+        sums = lax.psum(tuple(lo0) + tuple(up0), ("section", "batch")), lax.psum(tuple(lo1) + tuple(up1), ("section", "batch"))
+        sums = tuple(jnp.where(s == 0, a, b) for a, b in zip(*sums))
+    return (both(out0, out1), both(gin0, gin1)) + tuple(total[None] for total in sums)
 
 
 def solution(mesh):

time: 1300 us -> 596 us (0.46)
  waiting for transfers between devices: 641 us -> 2.94 us
  Pallas kernels: 0 us -> 230 us
  matrix products: 372 us -> 164 us
  blocking collectives: 83.6 us -> 0 us
  between operations: 17.1 us -> 2.62 us
    psum x1 -> x0, waiting for transfers between devices: 640 us -> none  [body(): summed = tuple(lax.psum(running, 'batch'))]
    pallas_call x0 -> x1, Pallas kernels: none -> 230 us  [reduce_grads(): pl.pallas_call(functools.partial(reduce_kernel, tuple(sc)), out_shape=(bl...]
    psum x1 -> x0, blocking collectives: 83.6 us -> none  [body(): summed = tuple(lax.psum(running, 'batch'))]
    dot_general x36 -> x12, matrix products: 111 us -> 36.4 us  [product(): return jnp.dot(left_side, right_side, preferred_element_type=jnp.float32)]
    dot_general x18 -> x12, matrix products: 74.1 us -> 31.8 us  [product_left(): lax.dot_general(left_side, right_side, (((0,), (0,)), ((), ())), preferre...]
    sub x3 -> x0, matrix products: 30.8 us -> none  [layer_forward(): exponent = jnp.exp(scores - row_peak)]
    dot_general x6 -> x2, matrix products: 32.4 us -> 9.09 us  [layer_forward(): jnp.einsum('hqk,khd->qhd', probs_low, values.reshape(row_count, HEADS, HE...]
    convert_element_type x0 -> x3, local copies, waits for them, and re-layouts: none -> 22.8 us  [the longest x2 13.2 us: grads_blocks(): low = lambda a: a.astype(jnp.bfloat16)]
  transfers between devices with their start and end apart: 5 -> 17, of which waited for: 2 -> 3; matrix products, arithmetic and copies ran while one was open for 9% -> 27% of each run, Pallas kernels for 0% -> 39%
where the time goes in v1:
time: 596 us; the launch traced here: 587 us
  Pallas kernels  230 us (39%)
  matrix products  164 us (28%)
  local copies, waits for them, and re-layouts  100 us (17%)
  other arithmetic  79.8 us (13%)
  starting transfers between devices  6.74 us (1%)
    pallas_call x1, Pallas kernels, reduce_grads(): pl.pallas_call(functools.partial(reduce_kernel, tuple(sc)), out_shape=(bl...  230 us
    unnamed x283, local copies, waits for them, and re-layouts  48.1 us
    dot_general x12, matrix products, product_right(): lax.dot_general(left_side, right_side, (((1,), (1,)), ((), ())), preferre...  38 us
    dot_general x12, matrix products, product(): return jnp.dot(left_side, right_side, preferred_element_type=jnp.float32)  36.4 us
    dot_general x12, matrix products, product_left(): lax.dot_general(left_side, right_side, (((0,), (0,)), ((), ())), preferre...  31.8 us
    dot_general x2, matrix products, lower_backward(): jnp.einsum('qhd,khd->hqk', grad_heads, values.reshape(heads_split), prefe...  19.2 us
    another operation x2, other arithmetic, body(): sums = outputs_of(*reduce_grads(jnp.stack([b0, b1]), jnp.stack([v0, v1])))  19.2 us
    dot_general x2, matrix products, lower_backward(): jnp.einsum('hqk,qhd->khd', probability.astype(jnp.bfloat16), grad_heads,...  19.1 us
  transfers between devices with their start and end apart: 17, of which 3 were waited for; matrix products, arithmetic and copies ran while one was open for 27% of the time, Pallas kernels for 39%

profile of v1, /device:TPU:0, one launch (start us, length us, event | category | flops | bytes accessed | tf_op | source)
XLA Modules:
  0.0 586.8 jit_solution(13832627270226644567)
XLA Ops:
  35.6 5.1 fusion.69
  45.0 5.3 multiply_convert_fusion.3
  81.3 6.8 %multiply_convert_fusion.2 = (bf16[512,3072]{1,0:T(8,128)(2,1)S(1)}, f32[512,3072]{1,0:T(8,128)S(1)}) fusion(f32[3072]{0:T(1024)S(1)} %get-tuple-element.82, bf16[768,3072]{1,0:T(8,128)(2,1)} %collective-permute-done.9, pred[]{:T(512)S(6)} %eq.12, bf16[1,768,3072]{2,1,0:T(8,128)(2,1)} %param.30, f32[512,768]{1,0:T(8,128)S(1)} %get-tuple-element.111, ...), kind=kOutput, calls=%fused_computation.36 | convolution fusion | flops 2429681664 | bytes 20469760 | tf_op jit(solution)/shard_map/dot_general | solution.py:322
  89.9 5.1 fusion.141
  98.9 8.5 %convert_reduce_fusion = (f32[3072]{0:T(1024)S(1)}, bf16[512,3072]{1,0:T(8,128)(2,1)}) fusion(f32[512,3072]{1,0:T(8,128)S(1)} %get-tuple-element.113, f32[3072]{0:T(1024)S(1)} %get-tuple-element.82, bf16[3072,768]{1,0:T(8,128)(2,1)} %collective-permute-done.11, pred[]{:T(512)S(6)} %eq.12, bf16[1,3072,768]{2,1,0:T(8,128)(2,1)S(1)} %bitcast.327, ...), kind=kOutput, calls=%fused_computation.32 | convolution fusion | flops 2439115776 | bytes 20471808 | tf_op jit(solution)/shard_map/dot_general | solution.py:332
  107.4 6.9 %multiply_reduce_fusion.2 = (f32[768]{0:T(1024)}, f32[512]{0:T(512)S(1)}, f32[512]{0:T(512)S(1)}, f32[768]{0:T(1024)}, f32[512,768]{1,0:T(8,128)S(1)}) fusion(f32[512,768]{1,0:T(8,128)S(1)} %get-tuple-element.111, f32[512]{0:T(512)S(1)} %add_rsqrt_fusion.1, f32[512]{0:T(512)S(1)} %broadcast_multiply_fusion.9, f32[768]{0:T(1024)S(1)} %get-tuple-element.86, ...), kind=kOutput, calls=%fused_computation.84 | convolution fusion | flops 2422208000 | bytes 17318912 | tf_op jit(solution)/shard_map/dot_general | solution.py:332
  120.0 9.6 %convert_reduce_fusion.6 = (f32[12,64]{1,0:T(8,128)}, bf16[12,64,512]{2,1,0:T(8,128)(2,1)}) fusion(bf16[512,12,64]{0,2,1:T(8,128)(2,1)} %bitcast.306, f32[12,512]{1,0:T(8,128)S(1)} %log_add_fusion.1, f32[12,512,512]{1,2,0:T(8,128)} %copy-done.1, pred[512,512]{0,1:T(8,128)(4,1)S(1)} %broadcast_compare_fusion), kind=kOutput, calls=%fused_computation.86 | convolution fusion | flops 416414976 | bytes 14445568 | tf_op jit(solution)/shard_map/hqk,qhd->khd/dot_general | solution.py:527
  129.6 9.6 %multiply_reduce_fusion.1 = (f32[12,512]{1,0:T(8,128)S(1)}, f32[12,512,512]{1,2,0:T(8,128)}) fusion(f32[12,512]{1,0:T(8,128)S(1)} %log_add_fusion.1, f32[12,512,512]{1,2,0:T(8,128)} %copy-done.1, pred[512,512]{0,1:T(8,128)(4,1)S(1)} %broadcast_compare_fusion, bf16[512,12,64]{0,2,1:T(8,128)(2,1)S(1)} %bitcast.307, bf16[512,12,64]{0,2,1:T(8,128)(2,1)S(1)} %bitcast.305), kind=kOutput, calls=%fused_computation.5 | convolution fusion | flops 418375680 | bytes 27049984 | tf_op jit(solution)/shard_map/qhd,khd->hqk/dot_general | solution.py:495
  139.3 7.3 %multiply_convert_fusion.1 = bf16[12,512,512]{1,2,0:T(8,128)(2,1)S(1)} fusion(f32[12,512,512]{1,2,0:T(8,128)} %get-tuple-element.118, f32[12,512]{1,0:T(8,128)S(1)} %get-tuple-element.117, f32[12,512]{1,0:T(8,128)S(1)} %log_add_fusion.1, f32[12,512,512]{1,2,0:T(8,128)S(1)} %bitcast.271, pred[512,512]{0,1:T(8,128)(4,1)S(1)} %broadcast_compare_fusion), kind=kLoop, calls=%fused_computation.4 | loop fusion | flops 18874368 | bytes 31768576 | tf_op jit(solution)/shard_map/convert_element_type | solution.py:499
  157.0 8.4 %convert_reduce_fusion.1 = (f32[3072]{0:T(1024)}, bf16[512,3072]{1,0:T(8,128)(2,1)S(1)}) fusion(f32[512,3072]{1,0:T(8,128)} %get-tuple-element.105, f32[3072]{0:T(1024)S(1)} %copy-done.89, bf16[3072,768]{1,0:T(8,128)(2,1)} %collective-permute-done.11, pred[]{:T(512)S(6)} %eq.12, bf16[1,3072,768]{2,1,0:T(8,128)(2,1)S(1)} %bitcast.329, ...), kind=kOutput, calls=%fused_computation.33 | convolution fusion | flops 2439115776 | bytes 20471808 | tf_op jit(solution)/shard_map/dot_general | solution.py:332
  175.2 9.6 %convert_reduce_fusion.10 = (f32[12,64]{1,0:T(8,128)}, bf16[12,64,512]{2,1,0:T(8,128)(2,1)}) fusion(bf16[512,12,64]{0,2,1:T(8,128)(2,1)} %bitcast.308, f32[12,512]{1,0:T(8,128)S(1)} %log_add_fusion, f32[12,512,512]{1,2,0:T(8,128)} %copy-done, pred[512,512]{0,1:T(8,128)(4,1)S(1)} %broadcast_compare_fusion), kind=kOutput, calls=%fused_computation.91 | convolution fusion | flops 416414976 | bytes 14445568 | tf_op jit(solution)/shard_map/hqk,qhd->khd/dot_general | solution.py:527
  184.8 9.6 %multiply_reduce_fusion = (f32[12,512]{1,0:T(8,128)S(1)}, f32[12,512,512]{1,2,0:T(8,128)}) fusion(f32[12,512]{1,0:T(8,128)S(1)} %log_add_fusion, f32[12,512,512]{1,2,0:T(8,128)} %copy-done, pred[512,512]{0,1:T(8,128)(4,1)S(1)} %broadcast_compare_fusion, bf16[512,12,64]{0,2,1:T(8,128)(2,1)S(1)} %bitcast.309, bf16[512,12,64]{0,2,1:T(8,128)(2,1)S(1)} %bitcast.303), kind=kOutput, calls=%fused_computation.2 | convolution fusion | flops 418375680 | bytes 27049984 | tf_op jit(solution)/shard_map/qhd,khd->hqk/dot_general | solution.py:495
  194.3 7.2 %multiply_convert_fusion = bf16[12,512,512]{1,2,0:T(8,128)(2,1)S(1)} fusion(f32[12,512,512]{1,2,0:T(8,128)} %get-tuple-element.122, f32[12,512]{1,0:T(8,128)S(1)} %get-tuple-element.121, f32[12,512]{1,0:T(8,128)S(1)} %log_add_fusion, f32[12,512,512]{1,2,0:T(8,128)S(1)} %bitcast.269, pred[512,512]{0,1:T(8,128)(4,1)S(1)} %broadcast_compare_fusion), kind=kLoop, calls=%fused_computation.1 | loop fusion | flops 18874368 | bytes 31768576 | tf_op jit(solution)/shard_map/convert_element_type | solution.py:499
  236.5 6.6 %copy.77 = bf16[768,3072]{0,1:T(8,128)(2,1)} copy(bf16[768,3072]{1,0:T(8,128)(2,1)} %convolution_convert_fusion) | data formatting | bytes 9437184 | tf_op jit(solution)/shard_map/convert_element_type | solution.py:555
  243.1 6.8 %copy.78 = bf16[768,4,768]{2,0,1:T(8,128)(2,1)} copy(bf16[768,4,768]{0,2,1:T(8,128)(2,1)} %bitcast.276) | data formatting | bytes 9437184 | tf_op jit(solution)/shard_map/reshape | solution.py:558
  264.6 6.6 %copy.75 = bf16[768,3072]{0,1:T(8,128)(2,1)} copy(bf16[768,3072]{1,0:T(8,128)(2,1)} %convolution_convert_fusion.2) | data formatting | bytes 9437184 | tf_op jit(solution)/shard_map/convert_element_type | solution.py:555
  271.3 6.6 %copy.76 = bf16[768,4,768]{2,0,1:T(8,128)(2,1)} copy(bf16[768,4,768]{0,2,1:T(8,128)(2,1)} %bitcast.277) | data formatting | bytes 9437184 | tf_op jit(solution)/shard_map/reshape | solution.py:558
  277.9 4.9 bitcast_dynamic-update-slice_fusion.1
  290.9 19.2 %pad_maximum_fusion.grads = bf16[2,12,768,768]{3,2,1,0:T(8,128)(2,1)} fusion(bf16[1,12,768,768]{3,2,1,0:T(8,128)(2,1)} %bitcast.273, bf16[1,12,768,768]{3,2,1,0:T(8,128)(2,1)} %bitcast.274), kind=kLoop, calls=%fused_computation | loop fusion | flops 14155776 | bytes 56623104 | tf_op jit(solution)/shard_map/stack | solution.py:608
  310.2 230.2 %shard_map.305 = (bf16[12,768,768]{2,1,0:T(8,128)(2,1)}, f32[16,768]{1,0:T(8,128)S(1)}, bf16[12,768,768]{2,1,0:T(8,128)(2,1)}) custom-call(bf16[2,12,768,768]{3,2,1,0:T(8,128)(2,1)} %pad_maximum_fusion.grads, f32[2,16,768]{2,1,0:T(8,128)S(1)} %pad_maximum_fusion.1.vec), custom_call_target="tpu_custom_call" | custom-call | tf_op jit(solution)/shard_map/pallas_call | solution.py:311
  540.5 8.6 %fusion.136 = (bf16[4,768,768]{2,1,0:T(8,128)(2,1)S(1)}, f32[768,4,768]{2,0,1:T(8,128)}) fusion(bf16[12,768,768]{2,1,0:T(8,128)(2,1)} %get-tuple-element.19), kind=kLoop, calls=%fused_computation.280 | loop fusion | flops 2359296 | bytes 23592960 | tf_op jit(solution)/shard_map/slice | solution.py:568
  553.5 6.2 %slice_convert_fusion = (f32[1,768,768]{2,1,0:T(8,128)}, f32[1,768,768]{2,1,0:T(8,128)}, f32[1,768,768]{2,1,0:T(8,128)}, f32[1,768,768]{2,1,0:T(8,128)}) fusion(bf16[12,768,768]{2,1,0:T(8,128)(2,1)} %get-tuple-element.19), kind=kLoop, calls=%fused_computation.161 | loop fusion | flops 2359296 | bytes 14155776 | tf_op jit(solution)/shard_map/convert_element_type | solution.py:567
  559.7 9.6 %copy.79 = f32[768,4,768]{0,2,1:T(8,128)} copy(f32[768,4,768]{2,0,1:T(8,128)} %get-tuple-element.65) | data formatting | bytes 18874368 | tf_op jit(solution)/shard_map/convert_element_type | solution.py:567
  569.3 9.7 %copy.80 = f32[1,768,3072]{2,1,0:T(8,128)} copy(f32[1,768,3072]{1,2,0:T(8,128)} %bitcast.272) | data formatting | bytes 18874368
  (446 shorter events, 170.3 us)
Async XLA Ops:
  1.4 7.6 %collective-permute-start.14 = (f32[768]{0:T(1024)S(1)}, f32[768]{0:T(1024)S(1)}, u32[]{:S(2)}, u32[]{:S(2)}) collective-permute-start(f32[768]{0:T(1024)S(1)} %reduce.15), channel_id=1, source_target_pairs={{0,16},{16,0},{1,17},{17,1},{2,18},{18,2},{3,19},{19,3},{4,20},{20... | collective-permute-start | bytes 9224 | tf_op jit(solution)/shard_map/ppermute | solution.py:579
  2.6 7.2 %collective-permute-start.13 = (f32[768]{0:T(1024)S(1)}, f32[768]{0:T(1024)S(1)}, u32[]{:S(2)}, u32[]{:S(2)}) collective-permute-start(f32[768]{0:T(1024)S(1)} %reduce.14), channel_id=1, source_target_pairs={{0,16},{16,0},{1,17},{17,1},{2,18},{18,2},{3,19},{19,3},{4,20},{20... | collective-permute-start | bytes 9224 | tf_op jit(solution)/shard_map/ppermute | solution.py:579
  3.4 6.8 %collective-permute-start.12 = (f32[768]{0:T(1024)S(1)}, f32[768]{0:T(1024)S(1)}, u32[]{:S(2)}, u32[]{:S(2)}) collective-permute-start(f32[768]{0:T(1024)S(1)} %reduce.13), channel_id=1, source_target_pairs={{0,16},{16,0},{1,17},{17,1},{2,18},{18,2},{3,19},{19,3},{4,20},{20... | collective-permute-start | bytes 9224 | tf_op jit(solution)/shard_map/ppermute | solution.py:579
  3.9 12.5 %collective-permute-start.10 = (f32[3072]{0:T(1024)}, f32[3072]{0:T(1024)S(1)}, u32[]{:S(2)}, u32[]{:S(2)}) collective-permute-start(f32[3072]{0:T(1024)} %bitcast.321), channel_id=1, source_target_pairs={{0,16},{16,0},{1,17},{17,1},{2,18},{18,2},{3,19},{19,3},{4,20},{20... | collective-permute-start | bytes 36872 | tf_op jit(solution)/shard_map/ppermute | solution.py:579
  4.7 6.2 %collective-permute-start.6 = (f32[768]{0:T(1024)S(1)}, f32[768]{0:T(1024)S(1)}, u32[]{:S(2)}, u32[]{:S(2)}) collective-permute-start(f32[768]{0:T(1024)S(1)} %reduce.10), channel_id=1, source_target_pairs={{0,16},{16,0},{1,17},{17,1},{2,18},{18,2},{3,19},{19,3},{4,20},{20... | collective-permute-start | bytes 9224 | tf_op jit(solution)/shard_map/ppermute | solution.py:579
  9.0 2.3 collective-permute-start.1
  9.7 43.9 %copy-start.81 = (f32[768]{0:T(1024)}, f32[768]{0:T(1024)S(1)}, u32[]{:S(2)}) copy-start(f32[768]{0:T(1024)S(1)} %get-tuple-element.99) | copy-start | bytes 9220
  9.7 7.5 %collective-permute-start = (bf16[768,768]{1,0:T(8,128)(2,1)}, bf16[768,768]{1,0:T(8,128)(2,1)S(1)}, u32[]{:S(2)}, u32[]{:S(2)}) collective-permute-start(bf16[768,768]{1,0:T(8,128)(2,1)} %bitcast.295), channel_id=1, source_target_pairs={{0,16},{16,0},{1,17},{17,1},{2,18},{18,2},{3,19},{19,3},{4,20},{20... | collective-permute-start | bytes 3538952 | tf_op jit(solution)/shard_map/ppermute | solution.py:579
  10.2 2.4 collective-permute-start.3
  10.9 9.3 %collective-permute-start.2 = (bf16[768,768]{1,0:T(8,128)(2,1)}, bf16[768,768]{1,0:T(8,128)(2,1)S(1)}, u32[]{:S(2)}, u32[]{:S(2)}) collective-permute-start(bf16[768,768]{1,0:T(8,128)(2,1)} %bitcast.301), channel_id=1, source_target_pairs={{0,16},{16,0},{1,17},{17,1},{2,18},{18,2},{3,19},{19,3},{4,20},{20... | collective-permute-start | bytes 3538952 | tf_op jit(solution)/shard_map/ppermute | solution.py:579
  11.3 10.6 %collective-permute-start.4 = (bf16[768,768]{1,0:T(8,128)(2,1)}, bf16[768,768]{1,0:T(8,128)(2,1)S(1)}, u32[]{:S(2)}, u32[]{:S(2)}) collective-permute-start(bf16[768,768]{1,0:T(8,128)(2,1)} %bitcast.300), channel_id=1, source_target_pairs={{0,16},{16,0},{1,17},{17,1},{2,18},{18,2},{3,19},{19,3},{4,20},{20... | collective-permute-start | bytes 3538952 | tf_op jit(solution)/shard_map/ppermute | solution.py:579
  12.6 1.8 collective-permute-start.8
  14.4 1.7 collective-permute-start.7
  14.7 35.5 %copy-start.101 = (f32[768]{0:T(1024)}, f32[768]{0:T(1024)S(1)}, u32[]{:S(2)}) copy-start(f32[768]{0:T(1024)S(1)} %get-tuple-element.89) | copy-start | bytes 9220
  14.7 73.5 %copy-start.103 = (f32[768]{0:T(1024)}, f32[768]{0:T(1024)S(1)}, u32[]{:S(2)}) copy-start(f32[768]{0:T(1024)S(1)} %get-tuple-element.88) | copy-start | bytes 9220
  16.0 27.4 %collective-permute-start.9 = (bf16[768,3072]{1,0:T(8,128)(2,1)}, bf16[768,3072]{1,0:T(8,128)(2,1)}, u32[]{:S(2)}, u32[]{:S(2)}) collective-permute-start(bf16[768,3072]{1,0:T(8,128)(2,1)} %bitcast.330), channel_id=1, source_target_pairs={{0,16},{16,0},{1,17},{17,1},{2,18},{18,2},{3,19},{19,3},{4,20},{20... | collective-permute-start | bytes 14155784 | tf_op jit(solution)/shard_map/ppermute | solution.py:579
  16.4 24.3 %collective-permute-start.5 = (bf16[768,768]{1,0:T(8,128)(2,1)}, bf16[768,768]{1,0:T(8,128)(2,1)S(1)}, u32[]{:S(2)}, u32[]{:S(2)}) collective-permute-start(bf16[768,768]{1,0:T(8,128)(2,1)} %bitcast.294), channel_id=1, source_target_pairs={{0,16},{16,0},{1,17},{17,1},{2,18},{18,2},{3,19},{19,3},{4,20},{20... | collective-permute-start | bytes 3538952 | tf_op jit(solution)/shard_map/ppermute | solution.py:579
  17.3 26.2 %copy-start.88 = (f32[3072]{0:T(1024)}, f32[3072]{0:T(1024)S(1)}, u32[]{:S(2)}) copy-start(f32[3072]{0:T(1024)S(1)} %get-tuple-element.83) | copy-start | bytes 36868
  17.3 33.0 %collective-permute-start.11 = (bf16[3072,768]{1,0:T(8,128)(2,1)}, bf16[3072,768]{1,0:T(8,128)(2,1)}, u32[]{:S(2)}, u32[]{:S(2)}) collective-permute-start(bf16[3072,768]{1,0:T(8,128)(2,1)} %bitcast.323), channel_id=1, source_target_pairs={{0,16},{16,0},{1,17},{17,1},{2,18},{18,2},{3,19},{19,3},{4,20},{20... | collective-permute-start | bytes 14155784 | tf_op jit(solution)/shard_map/ppermute | solution.py:579
  81.0 33.4 %copy-start.25 = (f32[512,768]{1,0:T(8,128)}, f32[512,768]{1,0:T(8,128)S(1)}, u32[]{:S(2)}) copy-start(f32[512,768]{1,0:T(8,128)S(1)} %get-tuple-element.111) | copy-start | bytes 4718596
  81.3 33.0 %copy-start.93 = (f32[512]{0:T(512)}, f32[512]{0:T(512)S(1)}, u32[]{:S(2)}) copy-start(f32[512]{0:T(512)S(1)} %add_rsqrt_fusion.1) | copy-start | bytes 6148
  203.6 23.9 %copy-start.29 = (bf16[12,64,512]{2,1,0:T(8,128)(2,1)}, bf16[12,64,512]{2,1,0:T(8,128)(2,1)S(1)}, u32[]{:S(2)}) copy-start(bf16[12,64,512]{2,1,0:T(8,128)(2,1)S(1)} %multiply_convert_fusion.4) | copy-start | bytes 2359300
  225.2 354.9 %collective-permute-start.15 = (bf16[512,768]{1,0:T(8,128)(2,1)}, bf16[512,768]{1,0:T(8,128)(2,1)}, u32[]{:S(2)}, u32[]{:S(2)}) collective-permute-start(bf16[512,768]{1,0:T(8,128)(2,1)} %get-tuple-element.62), channel_id=1, source_target_pairs={{0,16},{16,0},{1,17},{17,1},{2,18},{18,2},{3,19},{19,3},{4,20},{20... | collective-permute-start | bytes 2359304 | tf_op jit(solution)/shard_map/ppermute | solution.py:602
  233.9 349.3 %collective-permute-start.16 = (bf16[512,768]{1,0:T(8,128)(2,1)}, bf16[512,768]{1,0:T(8,128)(2,1)}, u32[]{:S(2)}, u32[]{:S(2)}) collective-permute-start(bf16[512,768]{1,0:T(8,128)(2,1)} %get-tuple-element.135), channel_id=1, source_target_pairs={{0,16},{16,0},{1,17},{17,1},{2,18},{18,2},{3,19},{19,3},{4,20},{20... | collective-permute-start | bytes 2359304 | tf_op jit(solution)/shard_map/ppermute | solution.py:602
  (131 other events, 579.2 us)
